TPU v7x, 32 devices: a whole 2x2x4 slice. The times are simulated.
32 devices in a mesh: arc: 2 (over core), row: 2 (over x), col: 8 (over z, y).
Axes of the slice: x: 2, y: 2, z: 4, core: 2. Of those that a mesh axis runs over, the one named last changes fastest.
Arguments:
- design: bfloat16 [6144, 6, 8, 128], P(('arc', 'row'), None, 'col'), may hold values from -0.076546554 to 0.076546554
- obs_weight: float32 [6144], P(('arc', 'row')), may hold values from 0.25 to 4
- prior: float32 [6, 8, 128], P(None, 'col'), may hold values from 0.3 to 3
Outputs:
- normal: float32 [24, 2, 128, 6, 8, 128], P(None, 'row', None, None, 'col')
- panel: float32 [24, 2, 128, 1024], P(None, 'row')
All inputs are finite; a program needn't handle non-finite values.
Results may differ from a plain program's by a relative error of at most 0.0012.
Values may be sent and summed in bfloat16 or wider, within the bound.
No kernel may reach another device: no remote copies, remote signals or barrier semaphores. Data moves between devices by JAX's collectives and lax.ppermute only.
A program may use at most 128 MiB of HBM per device.

v0:
```python
import jax
import jax.numpy as jnp
from jax import lax
from jax.sharding import PartitionSpec as P


def body(design, obs_weight, prior):
    n_row = lax.axis_size("row")
    n_col = lax.axis_size("col")
    rows_dev, kc_tiles, single, tile = design.shape
    coeffs = kc_tiles * n_col * tile
    kt_rows = coeffs // tile // n_row
    local_cols = kc_tiles * tile
    weighted = (design.astype(jnp.float32) * obs_weight[:, None, None, None]).astype(jnp.bfloat16)
    weighted = weighted.reshape(rows_dev, local_cols)
    partial_gram = jnp.einsum(
        "rkct,rj->kctj",
        lax.all_gather(design, "col", axis=2, tiled=True),
        weighted,
        preferred_element_type=jnp.float32,
    )
    blocks = partial_gram.reshape(kt_rows, n_row, tile, local_cols)
    owned = lax.psum_scatter(blocks, "row", scatter_dimension=1, tiled=True)
    tiles = lax.psum(owned, "arc").reshape(kt_rows, tile, local_cols)
    row_id = lax.axis_index("row")
    col_id = lax.axis_index("col")
    tile_rows = jnp.arange(kt_rows, dtype=jnp.int32) * n_row + row_id
    tile_cols = jnp.arange(kc_tiles, dtype=jnp.int32) * n_col + col_id
    same = (tile_rows[:, None] == tile_cols[None, :]).astype(jnp.float32)
    identity = jnp.eye(tile, dtype=jnp.float32)
    added = (
        same[:, None, :, None]
        * identity[None, :, None, :]
        * prior.reshape(kc_tiles, tile)[None, None, :, :]
    )
    normal_tiles = tiles.reshape(kt_rows, tile, kc_tiles, tile) + added
    normal = normal_tiles.reshape(kt_rows, 1, tile, kc_tiles, 1, tile)
    leading = normal_tiles[:, :, 0, :].reshape(kt_rows * tile, tile)
    panel_rows = lax.all_gather(leading, "col", axis=1, tiled=True)
    width = panel_rows.shape[1]
    lead_tiles = width // (tile * n_row)
    top = panel_rows.reshape(kt_rows, 1, tile, width)[:lead_tiles]
    square = lax.all_gather(top, "row", axis=1, tiled=True).reshape(width, width)
    factor = jnp.linalg.cholesky(square)
    result = lax.linalg.triangular_solve(
        factor, panel_rows, left_side=False, lower=True, transpose_a=True
    )
    return (normal, result.reshape(kt_rows, 1, tile, width))


def solution(mesh):
    placed = (P(("arc", "row"), None, "col", None), P(("arc", "row")), P(None, "col", None))
    return jax.shard_map(
        body,
        mesh=mesh,
        in_specs=placed,
        out_specs=(P(None, "row", None, None, "col", None), P(None, "row", None, None)),
        check_vma=False,
    )
```

profile of v0, /device:TPU:1, one launch (start us, length us, event | category | flops | bytes accessed | tf_op | source)
XLA Modules:
  0.0 1579.1 jit_solution(5665817245630131414)
XLA Ops:
  12.6 361.5 %all-gather.4.cloned.1.call-done = bf16[1536,6,8,128]{3,0,2,1:T(8,128)(2,1)} async-done(((bf16[1536,6,1,128]{3,0,2,1:T(8,128)(2,1)}), bf16[1536,6,8,128]{3,0,2,1:T(8,128)(2,1)}) %all-gather.4.cloned.1.call-update) | async-done | bytes 18874384 | tf_op jit(solution)/shard_map/all_gather | solution.py:18
  374.1 21.2 %fusion.71 = f32[768,6,8,128]{3,0,2,1:T(8,128)} fusion(bf16[1536,768,1,1]{0,1,3,2:T(8,128)(2,1)} %bitcast.136, bf16[1536,6,8,128]{3,0,2,1:T(8,128)(2,1)} %all-gather.4.cloned.1.call-done), kind=kOutput, calls=%fused_computation.166 | convolution fusion | flops 14495514624 | bytes 40108032 | tf_op jit(solution)/shard_map/rkct,rj->kctj/dot_general | solution.py:16
  396.6 422.0 %all-reduce.7.cloned.1.call-done = f32[24,2,128,768]{2,3,1,0:T(8,128)} async-done(((f32[24,2,128,768]{2,3,1,0:T(8,128)}), f32[24,2,128,768]{2,3,1,0:T(8,128)}) %all-reduce.7.cloned.1.call-update) | async-done | bytes 18874384
  818.6 9.0 constant_dynamic-slice_fusion.1
  828.3 41.7 %all-reduce.5.cloned.1.call-done = f32[24,1,128,768]{2,3,1,0:T(8,128)} async-done(((f32[24,1,128,768]{2,3,1,0:T(8,128)}), f32[24,1,128,768]{2,3,1,0:T(8,128)}) %all-reduce.5.cloned.1.call-update) | async-done | bytes 9437200 | tf_op jit(solution)/shard_map/psum | solution.py:24
  873.4 177.0 %all-gather.6.cloned.1.call-done = f32[3072,1024]{1,0:T(8,128)} async-done(((f32[3072,128]{1,0:T(8,128)}), f32[3072,1024]{1,0:T(8,128)}) %all-gather.6.cloned.1.call-update) | async-done | bytes 12582928 | tf_op jit(solution)/shard_map/all_gather | solution.py:39
  1053.7 20.7 %copy.25 = f32[24,1,128,6,1,128]{5,4,3,2,1,0:T(1,128)} copy(f32[24,1,128,6,1,128]{2,5,3,0,4,1:T(8,128)} %bitcast.132) | data formatting | bytes 18874368 | tf_op jit(solution)/shard_map/reshape;reshape | solution.py:36
  1074.4 12.0 multiply_add_fusion
  1086.5 22.7 %all-gather.8.cloned.1.call-done = f32[4,2,128,1024]{3,2,0,1:T(8,128)} async-done(((f32[4,1,128,1024]{3,2,0,1:T(8,128)}), f32[4,2,128,1024]{3,2,0,1:T(8,128)}) %all-gather.8.cloned.1.call-update) | async-done | bytes 4194320 | tf_op jit(solution)/shard_map/all_gather | solution.py:43
  1135.0 11.7 cholesky.187
  1146.7 9.8 custom-call.62
  1162.9 11.9 cholesky.209
  1175.4 9.8 custom-call.63
  1188.6 11.7 cholesky.402
  1201.6 9.8 custom-call.64
  1214.9 11.9 cholesky.421
  1228.1 9.8 custom-call.65
  1241.3 11.7 cholesky.440
  1254.4 10.2 custom-call.66
  1267.9 11.7 cholesky.460
  1280.9 9.8 custom-call.67
  1293.7 11.9 cholesky.480
  1306.9 9.8 custom-call.68
  1319.3 11.7 cholesky.498
  1343.0 23.6 %while.1 = (s32[]{:T(128)}, f32[1024,1024]{1,0:T(8,128)}, s32[8,2]{0,1:T(2,128)S(1)}, f32[8,128,128]{2,1,0:T(8,128)S(1)}, s32[]{:T(128)}) while((s32[]{:T(128)}, f32[1024,1024]{1,0:T(8,128)}, s32[8,2]{0,1:T(2,128)S(1)}, f32[8,128,128]{2,1,0:T(8,128)S(1)}, s32[]{:T(128)}) %tuple.65), condition=%wide.while_cond, body=%wide.while_body.sunk | while | flops 2 | bytes 131189 | solution.py:45
  1366.5 79.0 %custom-call.69 = f32[8,128,128]{1,2,0:T(8,128)S(1)} custom-call(f32[8,128,128]{2,1,0:T(8,128)S(1)} %get-tuple-element.9), custom_call_target="InvertDiagBlocksLowerTriangular" | custom-call | tf_op jit(solution)/shard_map/triangular_solve | solution.py:45
  1467.2 9.7 fusion.15
  1480.4 13.1 fusion.18
  1497.9 15.1 convolution_subtract_fusion.3
  1515.9 17.5 %convolution_subtract_fusion = f32[3072,128]{1,0:T(8,128)S(1)} fusion(f32[3072,768]{0,1:T(8,128)S(1)} %get-tuple-element.32, f32[3072,1024]{1,0:T(8,128)} %all-gather.6.cloned.1.call-done, f32[1024,1024]{1,0:T(8,128)} %get-tuple-element.140), kind=kOutput, calls=%fused_computation.23 | convolution fusion | flops 3624271872 | bytes 12976128 | tf_op jit(solution)/shard_map/triangular_solve | solution.py:45
  1536.1 20.9 %convolution_subtract_fusion.2 = f32[3072,128]{1,0:T(8,128)S(1)} fusion(f32[3072,896]{0,1:T(8,128)S(1)} %get-tuple-element.28, f32[3072,1024]{1,0:T(8,128)} %all-gather.6.cloned.1.call-done, f32[1024,1024]{1,0:T(8,128)} %get-tuple-element.140), kind=kOutput, calls=%fused_computation.25 | convolution fusion | flops 4228251648 | bytes 14614528 | tf_op jit(solution)/shard_map/triangular_solve | solution.py:45
  1559.8 12.6 copy.31
  (112 shorter events, 140.7 us)
Async XLA Ops:
  7.2 3.6 copy-start.1
  7.2 367.0 %all-gather.4.cloned.1.call-start = ((), (), s32[]{:S(2)}) async-start(), calls=%async_computation | async-start | bytes 21233664 | tf_op jit(solution)/shard_map/all_gather | solution.py:18
  7.9 810.7 %all-reduce.7.cloned.1.call-start = ((), (), s32[]{:S(2)}) async-start(), calls=%async_computation.4 | async-start | bytes 37748736
  395.3 0.7 copy-start.3
  395.4 474.5 %all-reduce.5.cloned.1.call-start = ((), (), s32[]{:S(2)}) async-start(), calls=%async_computation.1 | async-start | bytes 18874368 | tf_op jit(solution)/shard_map/psum | solution.py:24
  827.6 0.7 copy-start.2
  827.6 222.8 %all-gather.6.cloned.1.call-start = ((), (), s32[]{:S(2)}) async-start(), calls=%async_computation.2 | async-start | bytes 14155776 | tf_op jit(solution)/shard_map/all_gather | solution.py:39
  873.3 235.8 %all-gather.8.cloned.1.call-start = ((), (), s32[]{:S(2)}) async-start(), calls=%async_computation.3 | async-start | bytes 6291456 | tf_op jit(solution)/shard_map/all_gather | solution.py:43
  1133.0 2.0 copy-start
Sparse Core Ops, SparseCore 0:
  9.5 364.5 all-gather.3
  395.5 423.0 all-reduce.6
  827.7 42.1 all-reduce.4
  873.4 176.9 all-gather.5
  1053.7 55.3 all-gather.7
where the time goes:
time: 1590 us; the launch traced here: 1580 us
  waiting for transfers between devices  1030 us (65%)
  other arithmetic  276 us (17%)
  matrix products  158 us (10%)
  local copies, waits for them, and re-layouts  99.4 us (6%)
  between operations  19.3 us (1%)
    unnamed x6, waiting for transfers between devices  423 us
    all_gather x1, waiting for transfers between devices, body(): lax.all_gather(design, 'col', axis=2, tiled=True)  361 us
    all_gather x1, waiting for transfers between devices, body(): panel_rows = lax.all_gather(leading, 'col', axis=1, tiled=True)  177 us
    another operation x30, other arithmetic, body(): factor = jnp.linalg.cholesky(square)  172 us
    another operation x15, matrix products, body(): lax.linalg.triangular_solve(factor, panel_rows, left_side=False, lower=Tr...  114 us
    another operation x3, other arithmetic, body(): lax.linalg.triangular_solve(factor, panel_rows, left_side=False, lower=Tr...  83.9 us
    psum x1, waiting for transfers between devices, body(): tiles = lax.psum(owned, 'arc').reshape(kt_rows, tile, local_cols)  41.7 us
  transfers between devices with their start and end apart: 5, of which 5 were waited for; matrix products, arithmetic and copies ran while one was open for 2% of the time, Pallas kernels for 0%

commit v1 on v0

v1 whole, which is shorter than its diff:
```python
import jax
import jax.numpy as jnp
from jax import lax
from jax.sharding import PartitionSpec as P

F32 = jnp.float32
BF16 = jnp.bfloat16


def ring_order(n):
    return list(range(0, n, 2)) + list(range(1, n, 2))[::-1]


def swap(x, axis, shift=1):
    n = lax.axis_size(axis)
    return lax.ppermute(x, axis, [(i, (i + shift) % n) for i in range(n)])


def gather_cols(x):
    n = lax.axis_size("col")
    order = ring_order(n)
    got = lax.all_gather(x, "col", axis=0, tiled=False, axis_index_groups=[order])
    return jnp.stack([got[order.index(c)] for c in range(n)])


def partial_sums(blocks, weights):
    n_row = lax.axis_size("row")
    r = lax.axis_index("row")
    by_owner = blocks.reshape((blocks.shape[0] // n_row, n_row) + blocks.shape[1:])

    def part(owner):
        mine = lax.dynamic_index_in_dim(by_owner, owner, 1, keepdims=False)
        return jnp.einsum("q...rt,jru->q...tju", mine, weights, preferred_element_type=F32)

    arrived = [
        swap(part((r + d) % n_row).astype(BF16), "row", d) for d in range(1, n_row)
    ]
    total = part(r)
    for x in arrived:
        total = total + x.astype(F32)
    return total


def body(design, obs_weight, prior):
    n_row = lax.axis_size("row")
    n_col = lax.axis_size("col")
    a = lax.axis_index("arc")
    r = lax.axis_index("row")
    c = lax.axis_index("col")
    rows, kc, _, t = design.shape
    q = n_col // n_row
    m = (kc - 1) // 2
    own = jnp.transpose(design[:, :, 0, :], (1, 0, 2))
    lead_own = gather_cols(own[0])
    priors = gather_cols(prior[0, 0])
    rest_own = gather_cols(own[1 + 2 * m :])
    other = swap(own, "arc")
    weight_other = swap(obs_weight, "arc")

    def weigh(x, w):
        return (x.astype(F32) * w[:, None]).astype(BF16)

    both_own = jnp.concatenate([own, other], axis=1)
    w2 = jnp.concatenate([obs_weight, weight_other])
    weighted = weigh(both_own, w2)
    share = lax.dynamic_slice_in_dim(both_own, 1 + m * a, m, 0)

    lead = jnp.concatenate([lead_own, swap(lead_own, "arc")], axis=1)
    lead_weighted = weigh(lead, w2)
    half = n_col // 2
    lead_half = lax.dynamic_slice_in_dim(lead, half * a, half, 0)
    square_half = jnp.einsum("crt,jru->ctju", lead_half, lead_weighted, preferred_element_type=F32)
    for_sum = square_half
    if n_row == 2:
        square_half = square_half + swap(for_sum, "row")
    else:
        square_half = lax.psum(for_sum, "row")
    square_other = swap(square_half, "arc")
    first = a == 0
    square = jnp.concatenate(
        [jnp.where(first, square_half, square_other), jnp.where(first, square_other, square_half)]
    )
    width = n_col * t
    square = square.reshape(width, width) + jnp.diag(priors.reshape(width))

    main = gather_cols(share)
    rest = jnp.concatenate([rest_own, swap(rest_own, "arc")], axis=2)
    rest_half = lax.dynamic_slice_in_dim(rest, half * a, half, 0)

    def whole(main_rows, half_rows):
        main_rows = jnp.swapaxes(main_rows, 0, 1)
        other_main = swap(main_rows, "arc")
        other_half = swap(half_rows, "arc")

        def in_order(x, y):
            return jnp.where(first, x, y), jnp.where(first, y, x)

        lo, hi = in_order(main_rows, other_main)
        halves = jnp.swapaxes(jnp.concatenate(in_order(half_rows, other_half), axis=0), 0, 1)
        return halves, lo, hi

    halved = jnp.concatenate([lead_half[:, None], rest_half], axis=1)
    n_main = partial_sums(main, weighted)
    n_half = partial_sums(halved, weighted)
    halves, lo, hi = whole(n_main, n_half)
    tiles = jnp.concatenate([halves[:1], lo, hi, halves[1:]], axis=0)
    tiles = tiles.reshape(kc * q, t, kc, t)
    tile_rows = jnp.arange(kc * q, dtype=jnp.int32) * n_row + r
    tile_cols = jnp.arange(kc, dtype=jnp.int32) * n_col + c
    same = (tile_rows[:, None] == tile_cols[None, :]).astype(F32)
    identity = jnp.eye(t, dtype=F32)
    added = same[:, None, :, None] * identity[None, :, None, :] * prior.reshape(kc, t)[None, None]
    normal = (tiles + added).reshape(kc * q, 1, t, kc, 1, t)

    p_main = partial_sums(main, lead_weighted)
    p_half = partial_sums(rest_half, lead_weighted)
    halves, lo, hi = whole(p_main, p_half)
    top = lax.dynamic_index_in_dim(square.reshape(q, n_row, t, width), r, 1, keepdims=False)
    panel_rows = jnp.concatenate(
        [top[None].reshape(1, q, t, width)]
        + [x.reshape(-1, q, t, width) for x in (lo, hi, halves)],
        axis=0,
    ).reshape(kc * q * t, width)
    factor = jnp.linalg.cholesky(square)
    result = lax.linalg.triangular_solve(
        factor, panel_rows, left_side=False, lower=True, transpose_a=True
    )
    return (normal, result.reshape(kc * q, 1, t, width))


def solution(mesh):
    placed = (P(("arc", "row"), None, "col", None), P(("arc", "row")), P(None, "col", None))
    return jax.shard_map(
        body,
        mesh=mesh,
        in_specs=placed,
        out_specs=(P(None, "row", None, None, "col", None), P(None, "row", None, None)),
        check_vma=False,
    )
```

time: 1590 us -> 856 us (0.54)
  waiting for transfers between devices: 1030 us -> 145 us
  matrix products: 158 us -> 214 us
  local copies, waits for them, and re-layouts: 99.4 us -> 138 us
  other arithmetic: 276 us -> 307 us
    all_gather x3, waiting for transfers between devices: 561 us -> 63 us  [gather_cols(): lax.all_gather(x, 'col', axis=0, tiled=False, axis_index_groups=[order])]
    unnamed x6 -> x3, waiting for transfers between devices: 423 us -> 0.73 us
    ppermute x0 -> x14, waiting for transfers between devices: none -> 81.6 us  [swap(): return lax.ppermute(x, axis, [(i, (i + shift) % n) for i in range(n)])]
    dot_general x1 -> x9, matrix products: 21.2 us -> 70.8 us  [the longest x8 63 us: part(): jnp.einsum('q...rt,jru->q...tju', mine, weights, preferred_element_type=F32)]
    psum x1 -> x0, waiting for transfers between devices: 41.7 us -> none  [body(): tiles = lax.psum(owned, 'arc').reshape(kt_rows, tile, local_cols)]
    unnamed x14 -> x72, local copies, waits for them, and re-layouts: 28.5 us -> 59.9 us
    concatenate x0 -> x8, other arithmetic: none -> 17 us  [the longest x1 5.31 us: body(): jnp.concatenate([top[None].reshape(1, q, t, width)] + [x.reshape(-1, q, t...]
    select_n x0 -> x5, other arithmetic: none -> 16.7 us  [the longest x4 14.8 us: in_order(): return (jnp.where(first, x, y), jnp.where(first, y, x))]
  transfers between devices with their start and end apart: 5 -> 17, of which waited for: 5 -> 6; matrix products, arithmetic and copies ran while one was open for 2% -> 56% of each run, Pallas kernels for 0% -> 0%
where the time goes in v1:
time: 856 us; the launch traced here: 847 us
  other arithmetic  307 us (36%)
  matrix products  214 us (25%)
  waiting for transfers between devices  145 us (17%)
  local copies, waits for them, and re-layouts  138 us (16%)
  between operations  20 us (2%)
  starting transfers between devices  13.3 us (2%)
  blocking collectives  10.8 us (1%)
    another operation x30, other arithmetic, body(): factor = jnp.linalg.cholesky(square)  168 us
    another operation x15, matrix products, body(): lax.linalg.triangular_solve(factor, panel_rows, left_side=False, lower=Tr...  117 us
    another operation x3, other arithmetic, body(): lax.linalg.triangular_solve(factor, panel_rows, left_side=False, lower=Tr...  85.2 us
    ppermute x14, waiting for transfers between devices, swap(): return lax.ppermute(x, axis, [(i, (i + shift) % n) for i in range(n)])  81.6 us
    all_gather x3, waiting for transfers between devices, gather_cols(): lax.all_gather(x, 'col', axis=0, tiled=False, axis_index_groups=[order])  63 us
    dot_general x8, matrix products, part(): jnp.einsum('q...rt,jru->q...tju', mine, weights, preferred_element_type=F32)  63 us
    unnamed x72, local copies, waits for them, and re-layouts  59.9 us
    another operation x40, local copies, waits for them, and re-layouts  28.8 us
  transfers between devices with their start and end apart: 17, of which 6 were waited for; matrix products, arithmetic and copies ran while one was open for 56% of the time, Pallas kernels for 0%

profile of v1, /device:TPU:1, one launch (start us, length us, event | category | flops | bytes accessed | tf_op | source)
XLA Modules:
  0.0 847.5 jit_solution(11135264874347916822)
XLA Ops:
  17.8 31.9 %all-gather.9.cloned.1.call-done = bf16[8,1536,128]{2,1,0:T(8,128)(2,1)} async-done(((bf16[1,1536,128]{2,1,0:T(8,128)(2,1)}), bf16[8,1536,128]{2,1,0:T(8,128)(2,1)}) %all-gather.9.cloned.1.call-update) | async-done | bytes 3145744 | tf_op jit(solution)/shard_map/all_gather | solution.py:22
  58.9 31.1 %all-gather.7.cloned.1.call-done = bf16[8,1536,128]{2,1,0:T(8,128)(2,1)} async-done(((bf16[1,1536,128]{2,1,0:T(8,128)(2,1)}), bf16[8,1536,128]{2,1,0:T(8,128)(2,1)}) %all-gather.7.cloned.1.call-update) | async-done | bytes 3145744 | tf_op jit(solution)/shard_map/all_gather | solution.py:22
  155.8 38.5 %collective-permute-done.4 = bf16[2,2,128,6,128]{4,2,3,1,0:T(8,128)(2,1)} collective-permute-done((bf16[2,2,128,6,128]{4,2,3,1,0:T(8,128)(2,1)}, bf16[2,2,128,6,128]{4,2,3,1,0:T(8,128)(2,1)}, u32[]{:S(2)}, u32[]{:S(2)}) %collective-permute-start.4) | collective-permute-done | bytes 786464 | tf_op jit(solution)/shard_map/ppermute | solution.py:16
  200.5 10.8 %all-gather.2 = f32[8,1,128]{2,1,0:T(1,128)S(1)} all-gather(f32[1,1,128]{2,1,0:T(1,128)S(1)} %slice-done.4), channel_id=4, replica_groups={{0,2,4,6,7,5,3,1},{8,10,12,14,15,13,11,9},{16,18,20,22,23,21,19,17},{24..., dimensions={0}, use_global_device_ids=true | all-gather | bytes 4608 | tf_op jit(solution)/shard_map/all_gather | solution.py:22
  253.3 11.7 %cholesky.186 = f32[128,128]{1,0:T(8,128)S(1)} custom-call(f32[128,128]{1,0:T(8,128)S(1)} %cholesky.511), custom_call_target="Cholesky" | custom-call | tf_op jit(solution)/shard_map/jit(cholesky)/cholesky | solution.py:124
  265.2 9.8 %custom-call.62 = f32[1,128,128]{1,2,0:T(8,128)S(1)} custom-call(f32[1,128,128]{2,1,0:T(8,128)S(1)} %get-tuple-element.92), custom_call_target="InvertDiagBlocksLowerTriangular" | custom-call | tf_op jit(solution)/shard_map/jit(cholesky)/cholesky | solution.py:124
  278.3 11.9 %cholesky.208 = f32[128,128]{1,0:T(8,128)S(1)} custom-call(f32[128,128]{1,0:T(8,128)S(1)} %cholesky.515), custom_call_target="Cholesky" | custom-call | tf_op jit(solution)/shard_map/jit(cholesky)/cholesky | solution.py:124
  290.3 9.8 %custom-call.63 = f32[1,128,128]{1,2,0:T(8,128)S(1)} custom-call(f32[1,128,128]{2,1,0:T(8,128)S(1)} %get-tuple-element.90), custom_call_target="InvertDiagBlocksLowerTriangular" | custom-call | tf_op jit(solution)/shard_map/jit(cholesky)/cholesky | solution.py:124
  305.6 11.7 %cholesky.400 = f32[128,128]{1,0:T(8,128)S(1)} custom-call(f32[128,128]{1,0:T(8,128)S(1)} %cholesky.520), custom_call_target="Cholesky" | custom-call | tf_op jit(solution)/shard_map/jit(cholesky)/cholesky | solution.py:124
  317.5 9.8 %custom-call.64 = f32[1,128,128]{1,2,0:T(8,128)S(1)} custom-call(f32[1,128,128]{2,1,0:T(8,128)S(1)} %get-tuple-element.88), custom_call_target="InvertDiagBlocksLowerTriangular" | custom-call | tf_op jit(solution)/shard_map/jit(cholesky)/cholesky | solution.py:124
  332.7 11.7 %cholesky.419 = f32[128,128]{1,0:T(8,128)S(1)} custom-call(f32[128,128]{1,0:T(8,128)S(1)} %cholesky.525), custom_call_target="Cholesky" | custom-call | tf_op jit(solution)/shard_map/jit(cholesky)/cholesky | solution.py:124
  344.6 9.8 %custom-call.65 = f32[1,128,128]{1,2,0:T(8,128)S(1)} custom-call(f32[1,128,128]{2,1,0:T(8,128)S(1)} %get-tuple-element.86), custom_call_target="InvertDiagBlocksLowerTriangular" | custom-call | tf_op jit(solution)/shard_map/jit(cholesky)/cholesky | solution.py:124
  359.3 11.9 %cholesky.438 = f32[128,128]{1,0:T(8,128)S(1)} custom-call(f32[128,128]{1,0:T(8,128)S(1)} %cholesky.530), custom_call_target="Cholesky" | custom-call | tf_op jit(solution)/shard_map/jit(cholesky)/cholesky | solution.py:124
  371.3 9.8 %custom-call.66 = f32[1,128,128]{1,2,0:T(8,128)S(1)} custom-call(f32[1,128,128]{2,1,0:T(8,128)S(1)} %get-tuple-element.84), custom_call_target="InvertDiagBlocksLowerTriangular" | custom-call | tf_op jit(solution)/shard_map/jit(cholesky)/cholesky | solution.py:124
  386.0 11.7 %cholesky.458 = f32[128,128]{1,0:T(8,128)S(1)} custom-call(f32[128,128]{1,0:T(8,128)S(1)} %cholesky.535), custom_call_target="Cholesky" | custom-call | tf_op jit(solution)/shard_map/jit(cholesky)/cholesky | solution.py:124
  397.9 9.8 %custom-call.67 = f32[1,128,128]{1,2,0:T(8,128)S(1)} custom-call(f32[1,128,128]{2,1,0:T(8,128)S(1)} %get-tuple-element.82), custom_call_target="InvertDiagBlocksLowerTriangular" | custom-call | tf_op jit(solution)/shard_map/jit(cholesky)/cholesky | solution.py:124
  412.2 11.7 %cholesky.478 = f32[128,128]{1,0:T(8,128)S(1)} custom-call(f32[128,128]{1,0:T(8,128)S(1)} %cholesky.540), custom_call_target="Cholesky" | custom-call | tf_op jit(solution)/shard_map/jit(cholesky)/cholesky | solution.py:124
  424.0 9.8 %custom-call.68 = f32[1,128,128]{1,2,0:T(8,128)S(1)} custom-call(f32[1,128,128]{2,1,0:T(8,128)S(1)} %get-tuple-element.80), custom_call_target="InvertDiagBlocksLowerTriangular" | custom-call | tf_op jit(solution)/shard_map/jit(cholesky)/cholesky | solution.py:124
  459.7 9.9 %fusion.58 = bf16[4,2,128,8,128]{2,4,3,1,0:T(8,128)(2,1)} fusion(bf16[4,2,2,3072,128]{4,3,2,1,0:T(8,128)(2,1)S(1)} %bitcast.345, s32[]{:T(128)S(6)} %select_n.113, bf16[8,1536,128]{2,1,0:T(8,128)(2,1)} %collective-permute-done, bf16[8,1536,128]{2,1,0:T(8,128)(2,1)} %slice_dynamic-update-slice_fusion, f32[3072]{0:T(1024)S(1)} %constant_dynamic-update-slice_fusion.28), kind=kOutput, calls=%fused_computation.89 | convolution fusion | flops 6462373888 | bytes 14692356 | tf_op jit(solution)/shard_map/q...rt,jru->q...tju/dot_general | solution.py:33
  472.6 11.7 %cholesky.496 = f32[128,128]{1,0:T(8,128)S(1)} custom-call(f32[128,128]{1,0:T(8,128)S(1)} %convolution_subtract_fusion.11), custom_call_target="Cholesky" | custom-call | tf_op jit(solution)/shard_map/jit(cholesky)/cholesky | solution.py:124
  497.0 8.7 %add_bitcast_fusion.1 = f32[2,4,128,6,128]{4,2,3,0,1:T(8,128)S(1)} fusion(bf16[4,2,128,6,128]{4,2,3,1,0:T(8,128)(2,1)} %collective-permute-done.6, bf16[4,2,2,3072,128]{4,3,2,1,0:T(8,128)(2,1)} %bitcast.346, s32[]{:T(128)S(6)} %select_n.111, bf16[6,1536,128]{2,1,0:T(8,128)(2,1)S(1)} %copy-done.17, bf16[6,1536,128]{2,1,0:T(8,128)(2,1)S(1)} %bitcast.343, ...), kind=kOutput, calls=%fused_computation.83 | convolution fusion | flops 4847566848 | bytes 15740932 | tf_op jit(solution)/shard_map/q...rt,jru->q...tju/dot_general | solution.py:33
  506.5 33.3 %collective-permute-done.10 = bf16[4,2,128,8,128]{2,4,3,1,0:T(8,128)(2,1)} collective-permute-done((bf16[4,2,128,8,128]{2,4,3,1,0:T(8,128)(2,1)}, bf16[4,2,128,8,128]{2,4,3,1,0:T(8,128)(2,1)}, u32[]{:S(2)}, u32[]{:S(2)}) %collective-permute-start.10) | collective-permute-done | bytes 2097184 | tf_op jit(solution)/shard_map/ppermute | solution.py:16
  539.8 11.0 %add_bitcast_fusion = f32[2,4,128,8,128]{2,4,3,0,1:T(8,128)} fusion(bf16[4,2,128,8,128]{2,4,3,1,0:T(8,128)(2,1)} %collective-permute-done.10, bf16[4,2,2,3072,128]{4,3,2,1,0:T(8,128)(2,1)S(1)} %bitcast.349, s32[]{:T(128)S(6)} %select_n.111, bf16[8,1536,128]{2,1,0:T(8,128)(2,1)} %collective-permute-done, ...), kind=kOutput, calls=%fused_computation.61 | convolution fusion | flops 6463422464 | bytes 18886660 | tf_op jit(solution)/shard_map/q...rt,jru->q...tju/dot_general | solution.py:33
  551.6 28.9 %while.1 = (s32[]{:T(128)}, f32[1024,1024]{0,1:T(8,128)}, s32[8,2]{0,1:T(2,128)S(1)}, f32[8,128,128]{2,1,0:T(8,128)}, s32[]{:T(128)}) while((s32[]{:T(128)}, f32[1024,1024]{0,1:T(8,128)}, s32[8,2]{0,1:T(2,128)S(1)}, f32[8,128,128]{2,1,0:T(8,128)}, s32[]{:T(128)}) %tuple.72), condition=%wide.while_cond, body=%wide.while_body.sunk | while | flops 2 | bytes 393329 | solution.py:125
  580.6 80.0 %custom-call.69 = f32[8,128,128]{1,2,0:T(8,128)} custom-call(f32[8,128,128]{2,1,0:T(8,128)} %get-tuple-element.9), custom_call_target="InvertDiagBlocksLowerTriangular" | custom-call | tf_op jit(solution)/shard_map/triangular_solve | solution.py:125
  670.4 12.2 %copy.114 = f32[24,1,128,6,1,128]{5,4,3,2,1,0:T(1,128)} copy(f32[24,1,128,6,1,128]{5,2,4,3,1,0:T(8,128)} %multiply_add_fusion) | data formatting | bytes 18874368
  736.1 9.5 %fusion.36 = f32[3072,128]{1,0:T(8,128)S(1)} fusion(f32[3072,128]{0,1:T(8,128)} %get-tuple-element.101, f32[3072,128]{0,1:T(8,128)S(1)} %get-tuple-element.100, f32[3072,128]{0,1:T(8,128)S(1)} %get-tuple-element.99, f32[3072,1024]{1,0:T(8,128)S(1)} %bitcast.320, f32[1024,1024]{0,1:T(8,128)} %get-tuple-element.153), kind=kOutput, calls=%fused_computation.68 | convolution fusion | flops 1814691840 | bytes 8060928 | tf_op jit(solution)/shard_map/triangular_solve | solution.py:125
  749.7 13.0 %fusion.39 = f32[3072,128]{1,0:T(8,128)} fusion(f32[3072,128]{0,1:T(8,128)} %get-tuple-element.102, f32[3072,128]{0,1:T(8,128)} %get-tuple-element.101, f32[3072,128]{0,1:T(8,128)S(1)} %get-tuple-element.100, f32[3072,128]{0,1:T(8,128)S(1)} %get-tuple-element.99, f32[3072,1024]{1,0:T(8,128)S(1)} %bitcast.321, f32[1024,1024]{0,1:T(8,128)} %get-tuple-element.153), kind=kOutput, calls=%fused_computation.69 | convolution fusion | flops 2421030912 | bytes 9699328 | tf_op jit(solution)/shard_map/triangular_solve | solution.py:125
  767.6 14.6 %convolution_subtract_fusion.3 = f32[3072,128]{1,0:T(8,128)S(1)} fusion(f32[3072,640]{0,1:T(8,128)S(1)} %get-tuple-element.62, f32[3072,1024]{1,0:T(8,128)S(1)} %bitcast.322, f32[1024,1024]{0,1:T(8,128)} %get-tuple-element.153), kind=kOutput, calls=%fused_computation.66 | convolution fusion | flops 3020292096 | bytes 11337728 | tf_op jit(solution)/shard_map/triangular_solve | solution.py:125
  785.6 17.1 %convolution_subtract_fusion = f32[3072,128]{1,0:T(8,128)S(1)} fusion(f32[3072,768]{0,1:T(8,128)S(1)} %get-tuple-element.58, f32[3072,1024]{1,0:T(8,128)S(1)} %bitcast.323, f32[1024,1024]{0,1:T(8,128)} %get-tuple-element.153), kind=kOutput, calls=%fused_computation.63 | convolution fusion | flops 3624271872 | bytes 12976128 | tf_op jit(solution)/shard_map/triangular_solve | solution.py:125
  805.4 20.0 %convolution_subtract_fusion.2 = f32[3072,128]{1,0:T(8,128)S(1)} fusion(f32[3072,896]{0,1:T(8,128)S(1)} %get-tuple-element.54, f32[3072,1024]{1,0:T(8,128)S(1)} %bitcast.324, f32[1024,1024]{0,1:T(8,128)} %get-tuple-element.153), kind=kOutput, calls=%fused_computation.65 | convolution fusion | flops 4228251648 | bytes 14614528 | tf_op jit(solution)/shard_map/triangular_solve | solution.py:125
  828.2 12.6 %copy.141 = f32[3072,1024]{1,0:T(8,128)} copy(f32[3072,1024]{0,1:T(8,128)} %convolution_dynamic-update-slice_fusion) | data formatting | bytes 25165824
  (267 shorter events, 310.5 us)
Async XLA Ops:
  7.2 42.6 %all-gather.9.cloned.1.call-start = ((), (), s32[]{:S(2)}) async-start(), calls=%async_computation.1 | async-start | bytes 3538944 | tf_op jit(solution)/shard_map/all_gather | solution.py:22
  9.3 80.7 %all-gather.7.cloned.1.call-start = ((), (), s32[]{:S(2)}) async-start(), calls=%async_computation | async-start | bytes 3538944 | tf_op jit(solution)/shard_map/all_gather | solution.py:22
  10.0 432.1 %all-gather.11.cloned.1.call-start = ((), (), s32[]{:S(2)}) async-start(), calls=%async_computation.2 | async-start | bytes 14155776 | tf_op jit(solution)/shard_map/all_gather | solution.py:22
  10.1 4.8 collective-permute-start.2
  55.0 49.3 %copy-start.20 = (f32[1536]{0:T(1024)S(1)}, f32[1536]{0:T(1024)}, u32[]{:S(2)}) copy-start(f32[1536]{0:T(1024)} %param.4) | copy-start | bytes 18436
  57.3 52.2 %collective-permute-start.1 = (bf16[8,1,1536,128]{3,2,0,1:T(8,128)(2,1)S(1)}, bf16[8,1,1536,128]{3,2,0,1:T(8,128)(2,1)}, u32[]{:S(2)}, u32[]{:S(2)}) collective-permute-start(bf16[8,1,1536,128]{3,2,0,1:T(8,128)(2,1)S(1)} %fusion.111), channel_id=1, source_target_pairs={{0,16},{16,0},{1,17},{17,1},{2,18},{18,2},{3,19},{19,3},{4,20},{20... | collective-permute-start | bytes 9437192 | tf_op jit(solution)/shard_map/ppermute | solution.py:16
  102.8 8.4 collective-permute-start
  104.3 5.2 collective-permute-start.3
  111.1 19.2 %copy-start.5 = (bf16[4,1,3072,128]{3,2,0,1:T(8,128)(2,1)}, bf16[4,1,3072,128]{3,2,0,1:T(8,128)(2,1)S(1)}, u32[]{:S(2)}) copy-start(bf16[4,1,3072,128]{3,2,0,1:T(8,128)(2,1)S(1)} %fusion.42) | copy-start | bytes 9437188
  118.9 29.4 %collective-permute-start.12 = (bf16[2,1,128,8,128]{2,4,3,0,1:T(8,128)(2,1)}, bf16[2,1,128,8,128]{2,4,3,0,1:T(8,128)(2,1)}, u32[]{:S(2)}, u32[]{:S(2)}) collective-permute-start(bf16[2,1,128,8,128]{2,4,3,0,1:T(8,128)(2,1)} %fusion.101), channel_id=1, source_target_pairs={{0,8},{8,0},{1,9},{9,1},{2,10},{10,2},{3,11},{11,3},{4,12},{12,4},... | collective-permute-start | bytes 1572872 | tf_op jit(solution)/shard_map/ppermute | solution.py:16
  130.0 81.2 %collective-permute-start.8 = (f32[4,128,8,128]{1,3,2,0:T(8,128)}, f32[4,128,8,128]{1,3,2,0:T(8,128)}, u32[]{:S(2)}, u32[]{:S(2)}) collective-permute-start(f32[4,128,8,128]{1,3,2,0:T(8,128)} %fusion.22), channel_id=1, source_target_pairs={{0,8},{8,0},{1,9},{9,1},{2,10},{10,2},{3,11},{11,3},{4,12},{12,4},... | collective-permute-start | bytes 6291464 | tf_op jit(solution)/shard_map/ppermute | solution.py:16
  144.4 49.9 %collective-permute-start.4 = (bf16[2,2,128,6,128]{4,2,3,1,0:T(8,128)(2,1)}, bf16[2,2,128,6,128]{4,2,3,1,0:T(8,128)(2,1)}, u32[]{:S(2)}, u32[]{:S(2)}) collective-permute-start(bf16[2,2,128,6,128]{4,2,3,1,0:T(8,128)(2,1)} %fusion.83), channel_id=1, source_target_pairs={{0,8},{8,0},{1,9},{9,1},{2,10},{10,2},{3,11},{11,3},{4,12},{12,4},... | collective-permute-start | bytes 2359304 | tf_op jit(solution)/shard_map/ppermute | solution.py:16
  148.3 45.9 %copy-start.10 = (bf16[1536,6,1,128]{3,0,2,1:T(8,128)(2,1)S(1)}, bf16[1536,6,1,128]{3,0,2,1:T(8,128)(2,1)}, u32[]{:S(2)}) copy-start(bf16[1536,6,1,128]{3,0,2,1:T(8,128)(2,1)} %param.3) | copy-start | bytes 7077892
  148.3 45.9 %copy-start.13 = (bf16[2,1,2,3072,128]{3,4,2,0,1:T(8,128)(2,1)S(1)}, bf16[2,1,2,3072,128]{3,4,2,0,1:T(8,128)(2,1)}, u32[]{:S(2)}) copy-start(bf16[2,1,2,3072,128]{3,4,2,0,1:T(8,128)(2,1)} %copy.80) | copy-start | bytes 9437188
  148.3 45.9 %copy-start.15 = (bf16[6,1536,128]{2,1,0:T(8,128)(2,1)S(1)}, bf16[6,1536,128]{2,1,0:T(8,128)(2,1)}, u32[]{:S(2)}) copy-start(bf16[6,1536,128]{2,1,0:T(8,128)(2,1)} %copy-done.14) | copy-start | bytes 7077892
  154.8 45.6 %slice-start.4 = ((f32[6,1,128]{2,1,0:T(1,128)}), f32[1,1,128]{2,1,0:T(1,128)S(1)}, s32[]{:S(2)}) async-start(f32[6,1,128]{2,1,0:T(1,128)} %param.5), calls=%async_computation.7 | async-start | bytes 1024 | tf_op jit(solution)/shard_map/slice | solution.py:55
  154.9 61.3 %collective-permute-start.13 = (f32[2,1,128,8,128]{2,4,3,0,1:T(8,128)S(1)}, f32[2,1,128,8,128]{2,4,3,0,1:T(8,128)}, u32[]{:S(2)}, u32[]{:S(2)}) collective-permute-start(f32[2,1,128,8,128]{2,4,3,0,1:T(8,128)S(1)} %fusion.91), channel_id=1, source_target_pairs={{0,16},{16,0},{1,17},{17,1},{2,18},{18,2},{3,19},{19,3},{4,20},{20... | collective-permute-start | bytes 3145736 | tf_op jit(solution)/shard_map/ppermute | solution.py:16
  199.4 16.6 %copy-start.21 = (f32[6,1,128]{2,1,0:T(1,128)S(1)}, f32[6,1,128]{2,1,0:T(1,128)}, u32[]{:S(2)}) copy-start(f32[6,1,128]{2,1,0:T(1,128)} %param.5) | copy-start | bytes 9220
  199.4 22.5 %collective-permute-start.5 = (f32[2,2,128,6,128]{4,2,3,1,0:T(8,128)}, f32[2,2,128,6,128]{4,2,3,1,0:T(8,128)}, u32[]{:S(2)}, u32[]{:S(2)}) collective-permute-start(f32[2,2,128,6,128]{4,2,3,1,0:T(8,128)} %convert_add_fusion), channel_id=1, source_target_pairs={{0,16},{16,0},{1,17},{17,1},{2,18},{18,2},{3,19},{19,3},{4,20},{20... | collective-permute-start | bytes 4718600 | tf_op jit(solution)/shard_map/ppermute | solution.py:16
  213.7 12.9 %collective-permute-start.9 = (f32[4,128,8,128]{1,3,2,0:T(8,128)S(1)}, f32[4,128,8,128]{1,3,2,0:T(8,128)}, u32[]{:S(2)}, u32[]{:S(2)}) collective-permute-start(f32[4,128,8,128]{1,3,2,0:T(8,128)S(1)} %add.191), channel_id=1, source_target_pairs={{0,16},{16,0},{1,17},{17,1},{2,18},{18,2},{3,19},{19,3},{4,20},{20... | collective-permute-start | bytes 6291464 | tf_op jit(solution)/shard_map/ppermute | solution.py:16
  442.2 6.0 copy-start.4
  450.5 9.2 %copy-start.19 = (bf16[8,2,3072,128]{3,2,1,0:T(8,128)(2,1)}, bf16[8,2,3072,128]{3,2,1,0:T(8,128)(2,1)S(1)}, u32[]{:S(2)}) copy-start(bf16[8,2,3072,128]{3,2,1,0:T(8,128)(2,1)S(1)} %constant_dynamic-update-slice_fusion.1) | copy-start | bytes 37748740
  458.5 38.5 %collective-permute-start.6 = (bf16[4,2,128,6,128]{4,2,3,1,0:T(8,128)(2,1)}, bf16[4,2,128,6,128]{4,2,3,1,0:T(8,128)(2,1)}, u32[]{:S(2)}, u32[]{:S(2)}) collective-permute-start(bf16[4,2,128,6,128]{4,2,3,1,0:T(8,128)(2,1)} %fusion.65), channel_id=1, source_target_pairs={{0,8},{8,0},{1,9},{9,1},{2,10},{10,2},{3,11},{11,3},{4,12},{12,4},... | collective-permute-start | bytes 4718600 | tf_op jit(solution)/shard_map/ppermute | solution.py:16
  469.6 70.1 %collective-permute-start.10 = (bf16[4,2,128,8,128]{2,4,3,1,0:T(8,128)(2,1)}, bf16[4,2,128,8,128]{2,4,3,1,0:T(8,128)(2,1)}, u32[]{:S(2)}, u32[]{:S(2)}) collective-permute-start(bf16[4,2,128,8,128]{2,4,3,1,0:T(8,128)(2,1)} %fusion.58), channel_id=1, source_target_pairs={{0,8},{8,0},{1,9},{9,1},{2,10},{10,2},{3,11},{11,3},{4,12},{12,4},... | collective-permute-start | bytes 6291464 | tf_op jit(solution)/shard_map/ppermute | solution.py:16
  491.8 47.9 %slice-start.1 = ((s8[12582912]{0:T(1024)(128)(4,1)}), s8[4194304]{0:T(1024)(128)(4,1)S(1)}, s32[]{:S(2)}) async-start(s8[12582912]{0:T(1024)(128)(4,1)} %bitcast.347), calls=%async_computation.4 | async-start | bytes 8388608
  497.0 42.7 %slice-start.2 = ((s8[12582912]{0:T(1024)(128)(4,1)}), s8[4194304]{0:T(1024)(128)(4,1)S(1)}, s32[]{:S(2)}) async-start(s8[12582912]{0:T(1024)(128)(4,1)} %bitcast.347), calls=%async_computation.5 | async-start | bytes 8388608
  497.0 42.7 %slice-start.3 = ((s8[12582912]{0:T(1024)(128)(4,1)}), s8[4194304]{0:T(1024)(128)(4,1)S(1)}, s32[]{:S(2)}) async-start(s8[12582912]{0:T(1024)(128)(4,1)} %bitcast.347), calls=%async_computation.6 | async-start | bytes 8388608
  505.8 154.8 %collective-permute-start.7 = (f32[2,4,128,6,128]{4,2,3,0,1:T(8,128)S(1)}, f32[2,4,128,6,128]{4,2,3,0,1:T(8,128)}, u32[]{:S(2)}, u32[]{:S(2)}) collective-permute-start(f32[2,4,128,6,128]{4,2,3,0,1:T(8,128)S(1)} %add_bitcast_fusion.1), channel_id=1, source_target_pairs={{0,16},{16,0},{1,17},{17,1},{2,18},{18,2},{3,19},{19,3},{4,20},{20... | collective-permute-start | bytes 9437192 | tf_op jit(solution)/shard_map/ppermute | solution.py:16
  550.8 131.7 %collective-permute-start.11 = (f32[2,4,128,8,128]{2,4,3,0,1:T(8,128)}, f32[2,4,128,8,128]{2,4,3,0,1:T(8,128)}, u32[]{:S(2)}, u32[]{:S(2)}) collective-permute-start(f32[2,4,128,8,128]{2,4,3,0,1:T(8,128)} %add_bitcast_fusion), channel_id=1, source_target_pairs={{0,16},{16,0},{1,17},{17,1},{2,18},{18,2},{3,19},{19,3},{4,20},{20... | collective-permute-start | bytes 12582920 | tf_op jit(solution)/shard_map/ppermute | solution.py:16
  696.4 5.5 copy-start.7
  701.9 5.3 copy-start.18
  785.6 17.1 %copy-start.3 = (f32[3072,896]{0,1:T(8,128)S(1)}, f32[3072,896]{0,1:T(8,128)}, u32[]{:S(2)}) copy-start(f32[3072,896]{0,1:T(8,128)} %get-tuple-element.56) | copy-start | bytes 33030148
  (12 other events, 36.2 us)
Sparse Core Ops, SparseCore 0:
  10.1 39.5 all-gather.8
  51.8 38.0 all-gather.6
  91.5 127.1 all-gather.10
